TPU v7x, 512 devices: a whole 4x4x16 slice. The times are simulated.
512 devices in a mesh: body: 2 (over core), gx: 16 (over z), gy: 16 (over x, y).
Axes of the slice: x: 4, y: 4, z: 16, core: 2. Of those that a mesh axis runs over, the one named last changes fastest.
Arguments:
- disp: float32 [2, 3, 128, 512, 128], P('body', None, 'gx', 'gy'), may hold values from -4 to 4
- force: float32 [2, 3, 128, 512, 128], P('body', None, 'gx', 'gy'), may hold values from -12 to 12
- kappa: float32 [2, 128, 512, 128], P('body', 'gx', 'gy'), may hold values from 0.05 to 0.5
- sigma: float32 [2, 128, 512, 128], P('body', 'gx', 'gy'), may hold values from 0.2 to 1
- gap0: float32 [512, 128], P(('gx', 'gy')), may hold values from -3 to 3
- pressure: float32 [512, 128], P(('gx', 'gy')), may hold values from 0 to 1
- mortar: float32 [512, 128, 128], P(('gx', 'gy')), may hold values from -0.5 to 0.5
- partner: int32 [512], P(('gx', 'gy')), may hold values from 0 to 31
- active: int32 [512], P(('gx', 'gy')), may hold values 0 or 1
Outputs:
- increment: float32 [2, 3, 128, 512, 128], P('body', None, 'gx', 'gy')
- new_pressure: float32 [512, 128], P(('gx', 'gy'))
Inputs may be any that keep to these rules, and one draw needn't show every extreme that they name: partner numbers a master block of the same gy index: gx index times 2 plus the local block. 1 marks a block of the active contact set.
All inputs are finite; a program needn't handle non-finite values.
Results may differ from a plain program's by a relative error of at most 0.00015.
Values sent between devices are 32-bit elements; how exact they have to be, the bound alone decides.
No kernel may reach another device: no remote copies, remote signals or barrier semaphores. Data moves between devices by JAX's collectives and lax.ppermute only.
A program may use at most 64 MiB of HBM per device.

v0:
```python
import jax
import jax.numpy as jnp
from jax import lax
from jax.sharding import PartitionSpec as P

SBLK = 128
CG_ITERS = 2


def extended(block, sides, width):
    for axis, dim in sides:
        count = lax.axis_size(axis)
        forward = [(i, i + 1) for i in range(count - 1)]
        backward = [(target, source) for source, target in forward]
        low = lax.ppermute(
            lax.slice_in_dim(block, block.shape[dim] - width, None, axis=dim), axis, forward
        )
        high = lax.ppermute(lax.slice_in_dim(block, 0, width, axis=dim), axis, backward)
        block = jnp.concatenate([low, block, high], axis=dim)
    return block


def neighbours():
    result = []
    for first in (-1, 0, 1):
        for second in (-1, 0, 1):
            for third in (-1, 0, 1):
                if first != 0 or second != 0 or third != 0:
                    result.append((first, second, third))
    return result


def apply_stencil(field, padded, kappa, kappa_rim, sigma):
    sizes = field.shape[2:]
    total = sigma[:, None] * field
    for offset in neighbours():
        weight = 0.5 ** (abs(offset[0]) + abs(offset[1]) + abs(offset[2]) - 1)
        lower = [1 + offset[0], 1 + offset[1], 1 + offset[2]]
        bond = 0.5 * (
            kappa
            + kappa_rim[
                :,
                lower[0] : lower[0] + sizes[0],
                lower[1] : lower[1] + sizes[1],
                lower[2] : lower[2] + sizes[2],
            ]
        )
        near = padded[
            :,
            :,
            lower[0] : lower[0] + sizes[0],
            lower[1] : lower[1] + sizes[1],
            lower[2] : lower[2] + sizes[2],
        ]
        total = total + weight * bond[:, None] * (field - near)
    return total


def stencil(field, kappa, kappa_rim, sigma):
    padded = extended(field, (("gx", 2), ("gy", 3)), 1)
    padded = jnp.pad(padded, ((0, 0), (0, 0), (0, 0), (0, 0), (1, 1)))
    return apply_stencil(field, padded, kappa, kappa_rim, sigma)


def gap_of(field, selector, mortar):
    own = field[0, 2, :, :, 0].reshape(1, -1, SBLK)
    rows = lax.all_gather(own, ("body", "gx"), axis=0, tiled=True)
    row_count = lax.axis_size("gx")
    slave_own = lax.dynamic_index_in_dim(rows, lax.axis_index("gx"), 0, keepdims=False)
    master_row = rows[row_count:].reshape(-1, SBLK)
    picked = jnp.dot(selector, master_row, precision=lax.Precision.HIGHEST)
    pulled = jnp.einsum("bij,bj->bi", mortar, picked, precision=lax.Precision.HIGHEST)
    return -slave_own - pulled


def spread(traction, selector, mortar):
    pulled = jnp.einsum("bij,bi->bj", mortar, traction, precision=lax.Precision.HIGHEST)
    row_terms = -jnp.dot(selector.T, pulled, precision=lax.Precision.HIGHEST)
    share = lax.psum_scatter(row_terms, "gx", scatter_dimension=0, tiled=True)
    return jnp.where(lax.axis_index("body") == 0, -traction, share)


def add_surface(image, surface):
    return image.at[0, 2, :, :, 0].add(surface.reshape(image.shape[2], image.shape[3]))


def global_sum(value):
    return lax.psum(value, ("body", "gx", "gy"))


def on_device(disp, force, kappa, sigma, gap0, pressure, mortar, partner, active):
    kappa_rim = extended(kappa, (("gx", 1), ("gy", 2)), 1)
    kappa_rim = jnp.pad(kappa_rim, ((0, 0), (0, 0), (0, 0), (1, 1)))
    row_blocks = mortar.shape[0] * lax.axis_size("gx")
    selector = (partner[:, None] == jnp.arange(row_blocks, dtype=jnp.int32)[None, :]).astype(
        jnp.float32
    )
    flags = active.astype(jnp.float32)[:, None]
    gap = gap0 + gap_of(disp, selector, mortar)
    radius = jnp.sqrt(gap * gap + pressure * pressure + 0.01)
    complement = gap + pressure - radius
    slope_gap = 1.0 - gap / radius
    slope_press = 1.0 - pressure / radius
    divisor = slope_press + 0.5
    stiffness = flags * slope_gap / divisor
    excess = flags * complement / divisor
    rhs = force - stencil(disp, kappa, kappa_rim, sigma)
    rhs = add_surface(rhs, spread(flags * pressure - excess, selector, mortar))
    increment = jnp.zeros_like(rhs)
    residual = rhs
    direction = rhs
    norm_now = global_sum(jnp.sum(residual * residual))
    for step in range(CG_ITERS):
        image = stencil(direction, kappa, kappa_rim, sigma)
        image = add_surface(
            image, spread(stiffness * gap_of(direction, selector, mortar), selector, mortar)
        )
        alpha = norm_now / lax.psum(jnp.sum(direction * image), ("body", "gx", "gy"))
        increment = increment + alpha * direction
        residual = residual - alpha * image
        norm_next = global_sum(jnp.sum(residual * residual))
        direction = residual + norm_next / norm_now * direction
        norm_now = norm_next
    change = gap_of(increment, selector, mortar)
    new_press = flags * (pressure - (complement + slope_gap * change) / divisor)
    return (increment, new_press)


def solution(mesh):
    placed = (
        P("body", None, "gx", "gy", None),
        P("body", None, "gx", "gy", None),
        P("body", "gx", "gy", None),
        P("body", "gx", "gy", None),
        P(("gx", "gy"), None),
        P(("gx", "gy"), None),
        P(("gx", "gy"), None, None),
        P(("gx", "gy")),
        P(("gx", "gy")),
    )
    return jax.shard_map(
        on_device,
        mesh=mesh,
        in_specs=placed,
        out_specs=(P("body", None, "gx", "gy", None), P(("gx", "gy"), None)),
        check_vma=False,
    )
```

profile of v0, /device:TPU:1, one launch (start us, length us, event | category | flops | bytes accessed | tf_op | source)
XLA Modules:
  0.0 782.8 jit_solution(5270657747271295689)
XLA Ops:
  0.7 0.9 fusion.261
  1.5 4.4 collective-permute-start.4
  5.9 1.3 collective-permute-start.5
  7.2 0.7 fusion.263
  7.9 4.2 collective-permute-start
  12.1 1.3 collective-permute-start.1
  13.4 1.0 slice_reduce_fusion.2
  14.4 0.7 convert_element_type.10
  15.2 61.1 %all_gather.12 = f32[32,2,128]{2,1,0:T(2,128)S(1)} all-gather(f32[1,2,128]{2,1,0:T(2,128)S(1)} %reshape_squeeze.12), channel_id=1, replica_groups=mesh['body'=2,'gx'=16,'gy'=16] {'body','gx'}, dimensions={0}, use_global_device_ids=true | all-gather | bytes 33792 | tf_op jit(solution)/shard_map/all_gather | solution.py:67
  76.2 0.8 fusion.248
  77.4 0.8 divide_subtract_fusion
  78.4 0.9 convolution_negate_fusion.2
  79.3 1.3 dynamic-slice.22
  81.3 39.8 %all-reduce.4 = f32[32,128]{1,0:T(8,128)S(1)} all-reduce(f32[32,128]{1,0:T(8,128)S(1)} %convolution_negate_fusion.2), channel_id=2, replica_groups=mesh['body'=2,'gx'=16,'gy'=16] {'gx'}, use_global_device_ids=true, to_apply=%region_0.1.clone | all-reduce | flops 4096 | bytes 32768
  121.0 0.9 constant_dynamic-update-slice_fusion.1
  122.0 1.3 collective-permute-start.3
  123.3 4.0 collective-permute-start.2
  129.4 1.3 collective-permute-start.7
  130.7 4.2 collective-permute-start.6
  136.5 2.3 fusion.16
  139.1 1.3 collective-permute-start.9
  140.4 4.0 collective-permute-start.8
  144.5 70.0 %all_gather.13 = f32[32,2,128]{2,1,0:T(2,128)S(1)} all-gather(f32[1,2,128]{2,1,0:T(2,128)S(1)} %reshape_squeeze.13), channel_id=1, replica_groups=mesh['body'=2,'gx'=16,'gy'=16] {'body','gx'}, dimensions={0}, use_global_device_ids=true | all-gather | bytes 33792 | tf_op jit(solution)/shard_map/all_gather | solution.py:67
  216.2 39.1 %all-reduce.5 = f32[32,128]{1,0:T(8,128)S(1)} all-reduce(f32[32,128]{1,0:T(8,128)S(1)} %convolution_negate_fusion.1), channel_id=3, replica_groups=mesh['body'=2,'gx'=16,'gy'=16] {'gx'}, use_global_device_ids=true, to_apply=%region_3.4.clone | all-reduce | flops 4096 | bytes 32768
  255.3 1.3 collective-permute-start.11
  256.6 4.5 collective-permute-start.10
  261.1 0.9 reshape.409
  262.8 0.7 copy-done.9
  263.8 2.9 fusion.95
  266.9 0.8 multiply_reduce_fusion.2
  267.7 125.8 %all-reduce.7 = (f32[]{:T(128)}, f32[]{:T(128)}) all-reduce(f32[]{:T(128)} %get-tuple-element.39, f32[]{:T(128)} %get-tuple-element.38), channel_id=1, replica_groups=mesh['body'=2,'gx'=16,'gy'=16] {'body','gx','gy'}, use_global_device_ids=true, to_apply=%region_2.3 | all-reduce | flops 2 | bytes 16 | tf_op jit(solution)/shard_map/psum | solution.py:88
  394.8 0.7 multiply_reduce_fusion.1
  395.5 99.7 %psum.30 = f32[]{:T(128)} all-reduce(f32[]{:T(128)} %multiply_reduce_fusion.1), channel_id=1, replica_groups=mesh['body'=2,'gx'=16,'gy'=16] {'body','gx','gy'}, use_global_device_ids=true, to_apply=%region_7.8 | all-reduce | flops 1 | bytes 8 | tf_op jit(solution)/shard_map/psum | solution.py:88
  496.7 1.3 collective-permute-start.13
  498.0 4.0 collective-permute-start.12
  502.1 52.8 %all_gather.14 = f32[32,2,128]{2,1,0:T(2,128)S(1)} all-gather(f32[1,2,128]{2,1,0:T(2,128)S(1)} %reshape_squeeze.14), channel_id=1, replica_groups=mesh['body'=2,'gx'=16,'gy'=16] {'body','gx'}, dimensions={0}, use_global_device_ids=true | all-gather | bytes 33792 | tf_op jit(solution)/shard_map/all_gather | solution.py:67
  554.9 0.8 fusion.246
  556.1 0.7 fusion.242
  557.0 0.9 convolution_negate_fusion
  557.9 39.2 %all-reduce.6 = f32[32,128]{1,0:T(8,128)S(1)} all-reduce(f32[32,128]{1,0:T(8,128)S(1)} %convolution_negate_fusion), channel_id=4, replica_groups=mesh['body'=2,'gx'=16,'gy'=16] {'gx'}, use_global_device_ids=true, to_apply=%region_8.9.clone | all-reduce | flops 4096 | bytes 32768
  597.1 1.3 collective-permute-start.15
  598.4 4.2 collective-permute-start.14
  602.6 0.9 reshape.410
  604.2 0.7 copy-done.3
  605.4 2.9 fusion.41
  608.5 0.7 multiply_reduce_fusion
  609.2 117.7 %psum.31 = f32[]{:T(128)} all-reduce(f32[]{:T(128)} %multiply_reduce_fusion), channel_id=1, replica_groups=mesh['body'=2,'gx'=16,'gy'=16] {'body','gx','gy'}, use_global_device_ids=true, to_apply=%region_10.11 | all-reduce | flops 1 | bytes 8 | tf_op jit(solution)/shard_map/psum | solution.py:118
  728.5 53.1 %all_gather.15 = f32[32,2,128]{2,1,0:T(2,128)S(1)} all-gather(f32[1,2,128]{2,1,0:T(2,128)S(1)} %reshape_squeeze.15), channel_id=1, replica_groups=mesh['body'=2,'gx'=16,'gy'=16] {'body','gx'}, dimensions={0}, use_global_device_ids=true | all-gather | bytes 33792 | tf_op jit(solution)/shard_map/all_gather | solution.py:67
  (149 shorter events, 10.8 us)
Async XLA Ops:
  0.6 76.5 %copy-start = (f32[2,128,128]{2,1,0:T(8,128)S(1)}, f32[2,128,128]{2,1,0:T(8,128)}, u32[]{:S(2)}) copy-start(f32[2,128,128]{2,1,0:T(8,128)} %param.21) | copy-start | bytes 393220
  0.6 127.6 %copy-start.26 = (f32[1,8,32,128]{3,2,1,0:T(8,128)S(1)}, f32[1,8,32,128]{3,2,1,0:T(8,128)}, u32[]{:S(2)}) copy-start(f32[1,8,32,128]{3,2,1,0:T(8,128)} %param.17) | copy-start | bytes 393220
  1.5 127.2 %collective-permute-start.4 = (f32[1,3,1,32,128]{4,3,2,1,0:T(8,128)S(1)}, f32[1,3,1,32,128]{4,3,2,1,0:T(8,128)S(1)}, u32[]{:S(2)}, u32[]{:S(2)}) collective-permute-start(f32[1,3,1,32,128]{4,3,2,1,0:T(8,128)S(1)} %get-tuple-element.82), channel_id=1, source_target_pairs={{0,16},{16,32},{32,48},{48,64},{64,80},{80,96},{96,112},{112,128},... | collective-permute-start | bytes 147464 | tf_op jit(solution)/shard_map/ppermute | solution.py:15
  5.9 123.4 %collective-permute-start.5 = (f32[1,3,1,32,128]{4,3,2,1,0:T(8,128)S(1)}, f32[1,3,1,32,128]{4,3,2,1,0:T(8,128)S(1)}, u32[]{:S(2)}, u32[]{:S(2)}) collective-permute-start(f32[1,3,1,32,128]{4,3,2,1,0:T(8,128)S(1)} %get-tuple-element.81), channel_id=1, source_target_pairs={{16,0},{32,16},{48,32},{64,48},{80,64},{96,80},{112,96},{128,112},... | collective-permute-start | bytes 147464 | tf_op jit(solution)/shard_map/ppermute | solution.py:18
  7.9 113.1 %collective-permute-start = (f32[1,1,32,128]{3,2,1,0:T(8,128)S(1)}, f32[1,1,32,128]{3,2,1,0:T(8,128)S(1)}, u32[]{:S(2)}, u32[]{:S(2)}) collective-permute-start(f32[1,1,32,128]{3,2,1,0:T(8,128)S(1)} %get-tuple-element.97), channel_id=1, source_target_pairs={{0,16},{16,32},{32,48},{48,64},{64,80},{80,96},{96,112},{112,128},... | collective-permute-start | bytes 49160 | tf_op jit(solution)/shard_map/ppermute | solution.py:15
  12.1 109.8 %collective-permute-start.1 = (f32[1,1,32,128]{3,2,1,0:T(8,128)S(1)}, f32[1,1,32,128]{3,2,1,0:T(8,128)S(1)}, u32[]{:S(2)}, u32[]{:S(2)}) collective-permute-start(f32[1,1,32,128]{3,2,1,0:T(8,128)S(1)} %get-tuple-element.96), channel_id=1, source_target_pairs={{16,0},{32,16},{48,32},{64,48},{80,64},{96,80},{112,96},{128,112},... | collective-permute-start | bytes 49160 | tf_op jit(solution)/shard_map/ppermute | solution.py:18
  122.0 5.5 collective-permute-start.3
  123.3 4.7 collective-permute-start.2
  128.8 134.0 %copy-start.2 = (f32[8,32,128]{2,1,0:T(8,128)}, f32[8,32,128]{2,1,0:T(8,128)S(1)}, u32[]{:S(2)}) copy-start(f32[8,32,128]{2,1,0:T(8,128)S(1)} %get-tuple-element.66) | copy-start | bytes 393220
  129.4 5.8 collective-permute-start.7
  130.7 5.1 collective-permute-start.6
  135.0 3.8 copy-start.8
  135.0 3.8 copy-start.11
  135.1 3.7 copy-start.14
  135.1 3.7 copy-start.17
  135.1 3.7 copy-start.20
  135.1 3.7 copy-start.23
  135.1 127.6 %copy-start.4 = (f32[8,32,128]{2,1,0:T(8,128)}, f32[8,32,128]{2,1,0:T(8,128)S(1)}, u32[]{:S(2)}) copy-start(f32[8,32,128]{2,1,0:T(8,128)S(1)} %get-tuple-element.83) | copy-start | bytes 393220
  135.1 127.6 %copy-start.6 = (f32[8,32,128]{2,1,0:T(8,128)}, f32[8,32,128]{2,1,0:T(8,128)S(1)}, u32[]{:S(2)}) copy-start(f32[8,32,128]{2,1,0:T(8,128)S(1)} %get-tuple-element.84) | copy-start | bytes 393220
  135.1 1.2 copy-start.27
  135.1 1.4 copy-start.37
  136.5 78.0 %copy-start.39 = (s32[2]{0:T(128)S(1)}, s32[2]{0:T(128)}, u32[]{:S(2)}) copy-start(s32[2]{0:T(128)} %param.22) | copy-start | bytes 28
  136.5 78.5 %copy-start.38 = (f32[2,128]{1,0:T(2,128)S(1)}, f32[2,128]{1,0:T(2,128)}, u32[]{:S(2)}) copy-start(f32[2,128]{1,0:T(2,128)} %param.20) | copy-start | bytes 3076
  139.1 116.1 %collective-permute-start.9 = (f32[1,3,1,32,128]{4,3,2,1,0:T(8,128)S(1)}, f32[1,3,1,32,128]{4,3,2,1,0:T(8,128)S(1)}, u32[]{:S(2)}, u32[]{:S(2)}) collective-permute-start(f32[1,3,1,32,128]{4,3,2,1,0:T(8,128)S(1)} %get-tuple-element.80), channel_id=1, source_target_pairs={{16,0},{32,16},{48,32},{64,48},{80,64},{96,80},{112,96},{128,112},... | collective-permute-start | bytes 147464 | tf_op jit(solution)/shard_map/ppermute | solution.py:18
  140.4 114.8 %collective-permute-start.8 = (f32[1,3,1,32,128]{4,3,2,1,0:T(8,128)S(1)}, f32[1,3,1,32,128]{4,3,2,1,0:T(8,128)S(1)}, u32[]{:S(2)}, u32[]{:S(2)}) collective-permute-start(f32[1,3,1,32,128]{4,3,2,1,0:T(8,128)S(1)} %get-tuple-element.79), channel_id=1, source_target_pairs={{0,16},{16,32},{32,48},{48,64},{64,80},{80,96},{96,112},{112,128},... | collective-permute-start | bytes 147464 | tf_op jit(solution)/shard_map/ppermute | solution.py:15
  255.2 7.5 copy-start.32
  255.2 7.5 copy-start.33
  255.3 6.7 collective-permute-start.11
  256.6 5.4 collective-permute-start.10
  262.6 1.1 copy-start.21
  262.6 1.2 copy-start.24
  262.6 1.2 copy-start.28
  263.8 2.9 copy-start.36
  496.7 100.4 %collective-permute-start.13 = (f32[1,3,1,32,128]{4,3,2,1,0:T(8,128)S(1)}, f32[1,3,1,32,128]{4,3,2,1,0:T(8,128)S(1)}, u32[]{:S(2)}, u32[]{:S(2)}) collective-permute-start(f32[1,3,1,32,128]{4,3,2,1,0:T(8,128)S(1)} %get-tuple-element.78), channel_id=1, source_target_pairs={{16,0},{32,16},{48,32},{64,48},{80,64},{96,80},{112,96},{128,112},... | collective-permute-start | bytes 147464 | tf_op jit(solution)/shard_map/ppermute | solution.py:18
  498.0 99.1 %collective-permute-start.12 = (f32[1,3,1,32,128]{4,3,2,1,0:T(8,128)S(1)}, f32[1,3,1,32,128]{4,3,2,1,0:T(8,128)S(1)}, u32[]{:S(2)}, u32[]{:S(2)}) collective-permute-start(f32[1,3,1,32,128]{4,3,2,1,0:T(8,128)S(1)} %get-tuple-element.77), channel_id=1, source_target_pairs={{0,16},{16,32},{32,48},{48,64},{64,80},{80,96},{96,112},{112,128},... | collective-permute-start | bytes 147464 | tf_op jit(solution)/shard_map/ppermute | solution.py:15
  597.1 7.1 copy-start.30
  597.1 7.1 copy-start.31
  597.1 6.4 collective-permute-start.15
  598.4 5.1 collective-permute-start.14
  604.0 1.1 copy-start.13
  604.0 1.2 copy-start.16
  604.1 1.2 copy-start.19
  604.1 1.2 copy-start.22
  604.1 1.3 copy-start.25
  604.1 1.3 copy-start.29
  605.4 2.9 copy-start.35
  608.3 173.3 %copy-start.40 = (s32[2]{0:T(128)S(1)}, s32[2]{0:T(128)}, u32[]{:S(2)}) copy-start(s32[2]{0:T(128)} %param.22) | copy-start | bytes 28
  728.3 54.5 %copy-start.34 = (f32[1,3,8,32,128]{4,3,2,1,0:T(8,128)}, f32[1,3,8,32,128]{4,3,2,1,0:T(8,128)S(1)}, u32[]{:S(2)}) copy-start(f32[1,3,8,32,128]{4,3,2,1,0:T(8,128)S(1)} %multiply_add_fusion) | copy-start | bytes 1179652
  (9 other events, 8.9 us)
where the time goes:
time: 784 us; the launch traced here: 783 us
  blocking collectives  698 us (89%)
  starting transfers between devices  43.8 us (6%)
  other arithmetic  16.7 us (2%)
  local copies, waits for them, and re-layouts  10.8 us (1%)
    all_gather x4, blocking collectives, gap_of(): rows = lax.all_gather(own, ('body', 'gx'), axis=0, tiled=True)  237 us
    psum x2, blocking collectives, global_sum(): return lax.psum(value, ('body', 'gx', 'gy'))  226 us
    unnamed x3, blocking collectives  118 us
    psum x1, blocking collectives, on_device(): lax.psum(jnp.sum(direction * image), ('body', 'gx', 'gy'))  118 us
    ppermute x8, starting transfers between devices, extended(): lax.ppermute(lax.slice_in_dim(block, block.shape[dim] - width, None, axis...  33.4 us
  transfers between devices with their start and end apart: 16, of which 2 were waited for; matrix products, arithmetic and copies ran while one was open for 2% of the time, Pallas kernels for 0%

commit v1 on v0

--- a/solution.py
+++ b/solution.py
@@ -64,7 +64,10 @@
 
 def gap_of(field, selector, mortar):
     own = field[0, 2, :, :, 0].reshape(1, -1, SBLK)
-    rows = lax.all_gather(own, ("body", "gx"), axis=0, tiled=True)
+    devices = lax.axis_size(("body", "gx"))
+    blocks = jnp.stack([own for _ in range(devices)])
+    blocks = lax.all_to_all(blocks, ("body", "gx"), split_axis=0, concat_axis=0)
+    rows = jnp.concatenate(blocks, axis=0)
     row_count = lax.axis_size("gx")
     slave_own = lax.dynamic_index_in_dim(rows, lax.axis_index("gx"), 0, keepdims=False)
     master_row = rows[row_count:].reshape(-1, SBLK)

time: 784 us -> 644 us (0.82)
  blocking collectives: 698 us -> 475 us
  starting transfers between devices: 43.8 us -> 99.2 us
  waiting for transfers between devices: 1.14 us -> 21.9 us
    all_gather x4 -> x0, blocking collectives: 237 us -> none  [gap_of(): rows = lax.all_gather(own, ('body', 'gx'), axis=0, tiled=True)]
    all_to_all x0 -> x3, starting transfers between devices: none -> 56.9 us  [gap_of(): blocks = lax.all_to_all(blocks, ('body', 'gx'), split_axis=0, concat_axis=0)]
    all_to_all x0 -> x1, blocking collectives: none -> 19.4 us  [gap_of(): blocks = lax.all_to_all(blocks, ('body', 'gx'), split_axis=0, concat_axis=0)]
    all_to_all x0 -> x3, waiting for transfers between devices: none -> 15.5 us  [gap_of(): blocks = lax.all_to_all(blocks, ('body', 'gx'), split_axis=0, concat_axis=0)]
  transfers between devices with their start and end apart: 16 -> 19, of which waited for: 2 -> 6; matrix products, arithmetic and copies ran while one was open for 2% -> 3% of each run, Pallas kernels for 0% -> 0%
where the time goes in v1:
time: 644 us; the launch traced here: 642 us
  blocking collectives  475 us (74%)
  starting transfers between devices  99.2 us (15%)
  waiting for transfers between devices  21.9 us (3%)
  other arithmetic  18.6 us (3%)
  local copies, waits for them, and re-layouts  14.7 us (2%)
  matrix products  6.7 us (1%)
  between operations  6.52 us (1%)
    psum x2, blocking collectives, global_sum(): return lax.psum(value, ('body', 'gx', 'gy'))  220 us
    unnamed x3, blocking collectives  121 us
    psum x1, blocking collectives, on_device(): lax.psum(jnp.sum(direction * image), ('body', 'gx', 'gy'))  114 us
    all_to_all x3, starting transfers between devices, gap_of(): blocks = lax.all_to_all(blocks, ('body', 'gx'), split_axis=0, concat_axis=0)  56.9 us
    ppermute x8, starting transfers between devices, extended(): lax.ppermute(lax.slice_in_dim(block, block.shape[dim] - width, None, axis...  31.9 us
    all_to_all x1, blocking collectives, gap_of(): blocks = lax.all_to_all(blocks, ('body', 'gx'), split_axis=0, concat_axis=0)  19.4 us
    all_to_all x3, waiting for transfers between devices, gap_of(): blocks = lax.all_to_all(blocks, ('body', 'gx'), split_axis=0, concat_axis=0)  15.5 us
  transfers between devices with their start and end apart: 19, of which 6 were waited for; matrix products, arithmetic and copies ran while one was open for 3% of the time, Pallas kernels for 0%

profile of v1, /device:TPU:1, one launch (start us, length us, event | category | flops | bytes accessed | tf_op | source)
XLA Modules:
  0.0 642.3 jit_solution(15906893632857885120)
XLA Ops:
  0.7 0.8 fusion.263
  1.4 4.4 collective-permute-start
  5.8 0.8 fusion.261
  6.7 3.5 collective-permute-start.4
  10.2 1.3 collective-permute-start.5
  11.5 1.3 collective-permute-start.1
  12.8 0.9 constant_dynamic-update-slice_fusion.1
  13.7 3.5 collective-permute-done.1
  17.3 1.3 collective-permute-start.3
  18.6 4.0 collective-permute-start.2
  22.6 1.0 slice_reduce_fusion.2
  24.3 18.0 %all-to-all-start = ((f32[32,1,2,128]{3,2,1,0:T(2,128)}), f32[32,1,2,128]{3,2,1,0:T(2,128)}, u32[]{:S(2)}, u32[]{:S(2)}) async-start(f32[32,1,2,128]{3,2,1,0:T(2,128)} %stack.12), calls=%async_computation | async-start | bytes 65536 | tf_op jit(solution)/shard_map/all_to_all | solution.py:69
  42.3 1.2 convert_element_type.10
  43.5 1.3 dynamic-slice.26
  48.0 1.3 collective-permute-start.7
  49.3 4.0 collective-permute-start.6
  54.9 3.1 fusion.16
  59.3 0.8 divide_subtract_fusion
  60.3 0.9 convolution_negate_fusion.2
  61.2 42.5 %all-reduce.4 = f32[32,128]{1,0:T(8,128)S(1)} all-reduce(f32[32,128]{1,0:T(8,128)S(1)} %convolution_negate_fusion.2), channel_id=2, replica_groups=mesh['body'=2,'gx'=16,'gy'=16] {'gx'}, use_global_device_ids=true, to_apply=%region_0.1.clone | all-reduce | flops 4096 | bytes 32768
  104.2 1.3 collective-permute-start.9
  105.5 4.0 collective-permute-start.8
  109.5 1.1 collective-permute-done.8
  110.7 1.3 collective-permute-start.11
  112.0 4.1 collective-permute-start.10
  116.8 27.5 %all-to-all-start.1 = ((f32[32,1,2,128]{3,2,1,0:T(2,128)}), f32[32,1,2,128]{3,2,1,0:T(2,128)}, u32[]{:S(2)}, u32[]{:S(2)}) async-start(f32[32,1,2,128]{3,2,1,0:T(2,128)} %stack.13), calls=%async_computation.1 | async-start | bytes 65536 | tf_op jit(solution)/shard_map/all_to_all | solution.py:69
  146.1 2.9 fusion.95
  149.0 7.8 %all-to-all-done.1 = f32[32,1,2,128]{3,2,1,0:T(2,128)} async-done(((f32[32,1,2,128]{3,2,1,0:T(2,128)}), f32[32,1,2,128]{3,2,1,0:T(2,128)}, u32[]{:S(2)}, u32[]{:S(2)}) %all-to-all-start.1) | async-done | bytes 32800 | tf_op jit(solution)/shard_map/all_to_all | solution.py:69
  157.5 0.8 fusion.247
  158.7 1.3 fusion.243
  160.2 0.9 convolution_negate_fusion.1
  161.1 39.4 %all-reduce.5 = f32[32,128]{1,0:T(8,128)S(1)} all-reduce(f32[32,128]{1,0:T(8,128)S(1)} %convolution_negate_fusion.1), channel_id=3, replica_groups=mesh['body'=2,'gx'=16,'gy'=16] {'gx'}, use_global_device_ids=true, to_apply=%region_3.4.clone | all-reduce | flops 4096 | bytes 32768
  201.0 0.8 multiply_reduce_fusion.2
  201.7 120.5 %all-reduce.7 = (f32[]{:T(128)}, f32[]{:T(128)}) all-reduce(f32[]{:T(128)} %get-tuple-element.39, f32[]{:T(128)} %get-tuple-element.38), channel_id=1, replica_groups=mesh['body'=2,'gx'=16,'gy'=16] {'body','gx','gy'}, use_global_device_ids=true, to_apply=%region_2.3 | all-reduce | flops 2 | bytes 16 | tf_op jit(solution)/shard_map/psum | solution.py:91
  324.4 99.7 %psum.30 = f32[]{:T(128)} all-reduce(f32[]{:T(128)} %multiply_reduce_fusion.1), channel_id=1, replica_groups=mesh['body'=2,'gx'=16,'gy'=16] {'body','gx','gy'}, use_global_device_ids=true, to_apply=%region_7.8 | all-reduce | flops 1 | bytes 8 | tf_op jit(solution)/shard_map/psum | solution.py:91
  425.5 1.3 collective-permute-start.13
  426.8 4.0 collective-permute-start.12
  430.9 1.1 collective-permute-done.12
  432.0 1.3 collective-permute-start.15
  433.3 4.0 collective-permute-start.14
  438.1 11.4 %all-to-all-start.2 = ((f32[32,1,2,128]{3,2,1,0:T(2,128)}), f32[32,1,2,128]{3,2,1,0:T(2,128)}, u32[]{:S(2)}, u32[]{:S(2)}) async-start(f32[32,1,2,128]{3,2,1,0:T(2,128)} %stack.14), calls=%async_computation.2 | async-start | bytes 65536 | tf_op jit(solution)/shard_map/all_to_all | solution.py:69
  451.5 2.9 fusion.41
  454.4 7.7 %all-to-all-done.2 = f32[32,1,2,128]{3,2,1,0:T(2,128)} async-done(((f32[32,1,2,128]{3,2,1,0:T(2,128)}), f32[32,1,2,128]{3,2,1,0:T(2,128)}, u32[]{:S(2)}, u32[]{:S(2)}) %all-to-all-start.2) | async-done | bytes 32800 | tf_op jit(solution)/shard_map/all_to_all | solution.py:69
  462.7 0.8 fusion.246
  464.8 0.9 convolution_negate_fusion
  465.7 39.4 %all-reduce.6 = f32[32,128]{1,0:T(8,128)S(1)} all-reduce(f32[32,128]{1,0:T(8,128)S(1)} %convolution_negate_fusion), channel_id=4, replica_groups=mesh['body'=2,'gx'=16,'gy'=16] {'gx'}, use_global_device_ids=true, to_apply=%region_8.9.clone | all-reduce | flops 4096 | bytes 32768
  506.3 113.8 %psum.31 = f32[]{:T(128)} all-reduce(f32[]{:T(128)} %multiply_reduce_fusion), channel_id=1, replica_groups=mesh['body'=2,'gx'=16,'gy'=16] {'body','gx','gy'}, use_global_device_ids=true, to_apply=%region_10.11 | all-reduce | flops 1 | bytes 8 | tf_op jit(solution)/shard_map/psum | solution.py:121
  621.7 19.4 %all_to_all.20 = f32[32,1,2,128]{3,2,1,0:T(2,128)S(1)} all-to-all(f32[32,1,2,128]{3,2,1,0:T(2,128)S(1)} %stack.15), channel_id=1, replica_groups=mesh['body'=2,'gx'=16,'gy'=16] {'body','gx'}, dimensions={0} | all-to-all | bytes 65536 | tf_op jit(solution)/shard_map/all_to_all | solution.py:69
  (170 shorter events, 18.4 us)
Async XLA Ops:
  0.6 58.3 %copy-start = (f32[2,128,128]{2,1,0:T(8,128)S(1)}, f32[2,128,128]{2,1,0:T(8,128)}, u32[]{:S(2)}) copy-start(f32[2,128,128]{2,1,0:T(8,128)} %param.21) | copy-start | bytes 393220
  0.6 46.3 %copy-start.26 = (f32[1,8,32,128]{3,2,1,0:T(8,128)S(1)}, f32[1,8,32,128]{3,2,1,0:T(8,128)}, u32[]{:S(2)}) copy-start(f32[1,8,32,128]{3,2,1,0:T(8,128)} %param.17) | copy-start | bytes 393220
  1.4 11.4 %collective-permute-start = (f32[1,1,32,128]{3,2,1,0:T(8,128)S(1)}, f32[1,1,32,128]{3,2,1,0:T(8,128)S(1)}, u32[]{:S(2)}, u32[]{:S(2)}) collective-permute-start(f32[1,1,32,128]{3,2,1,0:T(8,128)S(1)} %get-tuple-element.97), channel_id=1, source_target_pairs={{0,16},{16,32},{32,48},{48,64},{64,80},{80,96},{96,112},{112,128},... | collective-permute-start | bytes 49160 | tf_op jit(solution)/shard_map/ppermute | solution.py:15
  6.7 40.8 %collective-permute-start.4 = (f32[1,3,1,32,128]{4,3,2,1,0:T(8,128)S(1)}, f32[1,3,1,32,128]{4,3,2,1,0:T(8,128)S(1)}, u32[]{:S(2)}, u32[]{:S(2)}) collective-permute-start(f32[1,3,1,32,128]{4,3,2,1,0:T(8,128)S(1)} %get-tuple-element.82), channel_id=1, source_target_pairs={{0,16},{16,32},{32,48},{48,64},{64,80},{80,96},{96,112},{112,128},... | collective-permute-start | bytes 147464 | tf_op jit(solution)/shard_map/ppermute | solution.py:15
  10.2 37.7 %collective-permute-start.5 = (f32[1,3,1,32,128]{4,3,2,1,0:T(8,128)S(1)}, f32[1,3,1,32,128]{4,3,2,1,0:T(8,128)S(1)}, u32[]{:S(2)}, u32[]{:S(2)}) collective-permute-start(f32[1,3,1,32,128]{4,3,2,1,0:T(8,128)S(1)} %get-tuple-element.81), channel_id=1, source_target_pairs={{16,0},{32,16},{48,32},{64,48},{80,64},{96,80},{112,96},{128,112},... | collective-permute-start | bytes 147464 | tf_op jit(solution)/shard_map/ppermute | solution.py:18
  11.5 5.8 collective-permute-start.1
  17.3 28.3 %copy-start.38 = (f32[1,1,32,128]{3,2,1,0:T(8,128)}, f32[1,1,32,128]{3,2,1,0:T(8,128)S(1)}, u32[]{:S(2)}) copy-start(f32[1,1,32,128]{3,2,1,0:T(8,128)S(1)} %collective-permute-done.1) | copy-start | bytes 49156
  17.3 28.2 %collective-permute-start.3 = (f32[1,10,1,128]{3,2,1,0:T(1,128)S(1)}, f32[1,10,1,128]{3,2,1,0:T(1,128)S(1)}, u32[]{:S(2)}, u32[]{:S(2)}) collective-permute-start(f32[1,10,1,128]{3,2,1,0:T(1,128)S(1)} %get-tuple-element.93), channel_id=1, source_target_pairs={{1,0},{2,1},{3,2},{4,3},{5,4},{6,5},{7,6},{8,7},{9,8},{10,9},{11,1... | collective-permute-start | bytes 15368 | tf_op jit(solution)/shard_map/ppermute | solution.py:18
  18.6 26.9 %collective-permute-start.2 = (f32[1,10,1,128]{3,2,1,0:T(1,128)S(1)}, f32[1,10,1,128]{3,2,1,0:T(1,128)S(1)}, u32[]{:S(2)}, u32[]{:S(2)}) collective-permute-start(f32[1,10,1,128]{3,2,1,0:T(1,128)S(1)} %get-tuple-element.92), channel_id=1, source_target_pairs={{0,1},{1,2},{2,3},{3,4},{4,5},{5,6},{6,7},{7,8},{8,9},{9,10},{10,1... | collective-permute-start | bytes 15368 | tf_op jit(solution)/shard_map/ppermute | solution.py:15
  24.3 33.8 %all-to-all-start = ((f32[32,1,2,128]{3,2,1,0:T(2,128)}), f32[32,1,2,128]{3,2,1,0:T(2,128)}, u32[]{:S(2)}, u32[]{:S(2)}) async-start(f32[32,1,2,128]{3,2,1,0:T(2,128)} %stack.12), calls=%async_computation | async-start | bytes 65536 | tf_op jit(solution)/shard_map/all_to_all | solution.py:69
  46.9 6.4 copy-start.39
  46.9 6.4 copy-start.41
  46.9 6.4 copy-start.43
  47.4 97.6 %copy-start.2 = (f32[8,32,128]{2,1,0:T(8,128)}, f32[8,32,128]{2,1,0:T(8,128)S(1)}, u32[]{:S(2)}) copy-start(f32[8,32,128]{2,1,0:T(8,128)S(1)} %get-tuple-element.66) | copy-start | bytes 393220
  47.4 7.2 %copy-start.36 = (f32[1,3,1,32,128]{4,3,2,1,0:T(8,128)}, f32[1,3,1,32,128]{4,3,2,1,0:T(8,128)S(1)}, u32[]{:S(2)}) copy-start(f32[1,3,1,32,128]{4,3,2,1,0:T(8,128)S(1)} %collective-permute-done.4) | copy-start | bytes 147460
  47.9 6.7 %copy-start.37 = (f32[1,3,1,32,128]{4,3,2,1,0:T(8,128)}, f32[1,3,1,32,128]{4,3,2,1,0:T(8,128)S(1)}, u32[]{:S(2)}) copy-start(f32[1,3,1,32,128]{4,3,2,1,0:T(8,128)S(1)} %collective-permute-done.5) | copy-start | bytes 147460
  48.0 5.6 collective-permute-start.7
  49.3 4.8 collective-permute-start.6
  53.4 1.2 copy-start.17
  53.5 1.2 copy-start.20
  53.5 1.2 copy-start.23
  53.5 4.6 copy-start.8
  53.5 4.6 copy-start.11
  53.5 4.5 copy-start.14
  53.5 91.6 %copy-start.4 = (f32[8,32,128]{2,1,0:T(8,128)}, f32[8,32,128]{2,1,0:T(8,128)S(1)}, u32[]{:S(2)}) copy-start(f32[8,32,128]{2,1,0:T(8,128)S(1)} %get-tuple-element.83) | copy-start | bytes 393220
  53.5 91.6 %copy-start.6 = (f32[8,32,128]{2,1,0:T(8,128)}, f32[8,32,128]{2,1,0:T(8,128)S(1)}, u32[]{:S(2)}) copy-start(f32[8,32,128]{2,1,0:T(8,128)S(1)} %get-tuple-element.84) | copy-start | bytes 393220
  53.5 1.4 copy-start.35
  54.9 3.9 copy-start.46
  54.9 4.4 copy-start.44
  54.9 4.4 copy-start.45
  104.2 5.3 collective-permute-start.9
  105.5 5.2 collective-permute-start.8
  109.5 35.5 %copy-start.32 = (f32[1,3,1,32,128]{4,3,2,1,0:T(8,128)}, f32[1,3,1,32,128]{4,3,2,1,0:T(8,128)S(1)}, u32[]{:S(2)}) copy-start(f32[1,3,1,32,128]{4,3,2,1,0:T(8,128)S(1)} %collective-permute-done.9) | copy-start | bytes 147460
  110.7 34.4 %copy-start.33 = (f32[1,3,1,32,128]{4,3,2,1,0:T(8,128)}, f32[1,3,1,32,128]{4,3,2,1,0:T(8,128)S(1)}, u32[]{:S(2)}) copy-start(f32[1,3,1,32,128]{4,3,2,1,0:T(8,128)S(1)} %collective-permute-done.8) | copy-start | bytes 147460
  110.7 33.6 %collective-permute-start.11 = (f32[1,3,10,1,128]{4,3,2,1,0:T(1,128)S(1)}, f32[1,3,10,1,128]{4,3,2,1,0:T(1,128)S(1)}, u32[]{:S(2)}, u32[]{:S(2)}) collective-permute-start(f32[1,3,10,1,128]{4,3,2,1,0:T(1,128)S(1)} %get-tuple-element.74), channel_id=1, source_target_pairs={{1,0},{2,1},{3,2},{4,3},{5,4},{6,5},{7,6},{8,7},{9,8},{10,9},{11,1... | collective-permute-start | bytes 46088 | tf_op jit(solution)/shard_map/ppermute | solution.py:18
  112.0 32.3 %collective-permute-start.10 = (f32[1,3,10,1,128]{4,3,2,1,0:T(1,128)S(1)}, f32[1,3,10,1,128]{4,3,2,1,0:T(1,128)S(1)}, u32[]{:S(2)}, u32[]{:S(2)}) collective-permute-start(f32[1,3,10,1,128]{4,3,2,1,0:T(1,128)S(1)} %get-tuple-element.73), channel_id=1, source_target_pairs={{0,1},{1,2},{2,3},{3,4},{4,5},{5,6},{6,7},{7,8},{8,9},{9,10},{10,1... | collective-permute-start | bytes 46088 | tf_op jit(solution)/shard_map/ppermute | solution.py:15
  116.8 40.0 %all-to-all-start.1 = ((f32[32,1,2,128]{3,2,1,0:T(2,128)}), f32[32,1,2,128]{3,2,1,0:T(2,128)}, u32[]{:S(2)}, u32[]{:S(2)}) async-start(f32[32,1,2,128]{3,2,1,0:T(2,128)} %stack.13), calls=%async_computation.1 | async-start | bytes 65536 | tf_op jit(solution)/shard_map/all_to_all | solution.py:69
  425.5 5.3 collective-permute-start.13
  426.8 5.2 collective-permute-start.12
  430.8 19.2 %copy-start.30 = (f32[1,3,1,32,128]{4,3,2,1,0:T(8,128)}, f32[1,3,1,32,128]{4,3,2,1,0:T(8,128)S(1)}, u32[]{:S(2)}) copy-start(f32[1,3,1,32,128]{4,3,2,1,0:T(8,128)S(1)} %collective-permute-done.13) | copy-start | bytes 147460
  432.0 18.1 %copy-start.31 = (f32[1,3,1,32,128]{4,3,2,1,0:T(8,128)}, f32[1,3,1,32,128]{4,3,2,1,0:T(8,128)S(1)}, u32[]{:S(2)}) copy-start(f32[1,3,1,32,128]{4,3,2,1,0:T(8,128)S(1)} %collective-permute-done.12) | copy-start | bytes 147460
  432.0 17.5 %collective-permute-start.15 = (f32[1,3,10,1,128]{4,3,2,1,0:T(1,128)S(1)}, f32[1,3,10,1,128]{4,3,2,1,0:T(1,128)S(1)}, u32[]{:S(2)}, u32[]{:S(2)}) collective-permute-start(f32[1,3,10,1,128]{4,3,2,1,0:T(1,128)S(1)} %get-tuple-element.70), channel_id=1, source_target_pairs={{1,0},{2,1},{3,2},{4,3},{5,4},{6,5},{7,6},{8,7},{9,8},{10,9},{11,1... | collective-permute-start | bytes 46088 | tf_op jit(solution)/shard_map/ppermute | solution.py:18
  433.3 16.2 %collective-permute-start.14 = (f32[1,3,10,1,128]{4,3,2,1,0:T(1,128)S(1)}, f32[1,3,10,1,128]{4,3,2,1,0:T(1,128)S(1)}, u32[]{:S(2)}, u32[]{:S(2)}) collective-permute-start(f32[1,3,10,1,128]{4,3,2,1,0:T(1,128)S(1)} %get-tuple-element.69), channel_id=1, source_target_pairs={{0,1},{1,2},{2,3},{3,4},{4,5},{5,6},{6,7},{7,8},{8,9},{9,10},{10,1... | collective-permute-start | bytes 46088 | tf_op jit(solution)/shard_map/ppermute | solution.py:15
  438.1 23.9 %all-to-all-start.2 = ((f32[32,1,2,128]{3,2,1,0:T(2,128)}), f32[32,1,2,128]{3,2,1,0:T(2,128)}, u32[]{:S(2)}, u32[]{:S(2)}) async-start(f32[32,1,2,128]{3,2,1,0:T(2,128)} %stack.14), calls=%async_computation.2 | async-start | bytes 65536 | tf_op jit(solution)/shard_map/all_to_all | solution.py:69
  450.2 1.3 copy-start.25
  450.2 1.3 copy-start.29
  505.4 135.7 %copy-start.47 = (s32[2]{0:T(128)S(1)}, s32[2]{0:T(128)}, u32[]{:S(2)}) copy-start(s32[2]{0:T(128)} %param.22) | copy-start | bytes 28
  621.5 20.8 %copy-start.34 = (f32[1,3,8,32,128]{4,3,2,1,0:T(8,128)}, f32[1,3,8,32,128]{4,3,2,1,0:T(8,128)S(1)}, u32[]{:S(2)}) copy-start(f32[1,3,8,32,128]{4,3,2,1,0:T(8,128)S(1)} %multiply_add_fusion) | copy-start | bytes 1179652
  (19 other events, 19.4 us)
